TPU v7x, 32 devices: a whole 2x2x4 slice. The times are simulated.
32 devices in a mesh: grid: 4 (over y, core), tile: 8 (over z, x).
Axes of the slice: x: 2, y: 2, z: 4, core: 2. Of those that a mesh axis runs over, the one named last changes fastest.
Arguments:
- rhs_local: bfloat16 [192, 49152], P(None, ('grid', 'tile')), may hold values from -6 to 6
- diag_inv: bfloat16 [96, 512, 512], P(('grid', 'tile')), may hold values from -1 to 2, as said below
- codes: bfloat16 [20480, 1536], P(('grid', 'tile')), may hold values from -127 to 127, as said below
- row_scales: float32 [20480], P(('grid', 'tile')), may hold values from 0 to 1, as said below
- sep_index: int32 [20480], P(('grid', 'tile')), may hold values from 0 to 2559, as said below
- live_rows: int32 [32], P(('grid', 'tile')), may hold values from 160 to 640, as said below
- rhs_sep: bfloat16 [192, 2560], P(None, 'tile'), may hold values from -6 to 6
- root_inv: bfloat16 [2560, 2560], P('tile'), may hold values from -1 to 2, as said below
Outputs:
- solution_local: bfloat16 [192, 49152], P(None, ('grid', 'tile'))
- solution_sep: float32 [192, 2560], P(None, 'tile')
Inputs may be any that keep to these rules, and one draw needn't show every extreme that they name: `diag_inv`: each block is upper triangular. `root_inv`: each block is upper triangular. `codes`: Integers. `row_scales`: Positive. `sep_index`: of each device's 640 entries, the j-th run of 80 consecutive entries lies in j * 320 to (j + 1) * 320 - 1, and the entries of one run are distinct. `live_rows`: some device has all 640 rows live.
All inputs are finite; a program needn't handle non-finite values.
Results may differ from a plain program's by a relative error of at most 0.0054.
Values may be sent and summed in bfloat16 or wider, within the bound.
A program may use at most 64 MiB of HBM per device.

v0:
```python
import jax
import jax.numpy as jnp
from jax import lax
from jax.sharding import PartitionSpec as P


def selector(offsets, share_len):
    columns = jnp.arange(share_len, dtype=jnp.int32)
    return (offsets[:, :, None] == columns[None, None, :]).astype(jnp.float32)


def on_device(rhs_local, diag_inv, codes, row_scales, sep_index, live_rows, rhs_sep, root_inv):
    rhs_count, local_len = rhs_local.shape
    per_dev, block_len = (diag_inv.shape[0], diag_inv.shape[1])
    coupled_rows = codes.shape[0]
    share_len, sep_len = root_inv.shape
    tile_count = lax.axis_size("tile")
    per_share = coupled_rows // tile_count
    pieces = []
    for block_pos in range(per_dev):
        columns = rhs_local[:, block_pos * block_len : (block_pos + 1) * block_len]
        pieces.append(jnp.dot(columns, diag_inv[block_pos], preferred_element_type=jnp.float32))
    forward_flat = jnp.concatenate(pieces, axis=1).astype(jnp.bfloat16)
    positions = jnp.arange(coupled_rows, dtype=jnp.int32)
    row_factor = row_scales * (positions < live_rows[0]).astype(jnp.float32)
    coupled = (
        lax.dot_general(
            forward_flat, codes, (((1,), (1,)), ((), ())), preferred_element_type=jnp.float32
        )
        * row_factor[None, :]
    )
    bases = (jnp.arange(tile_count, dtype=jnp.int32) * share_len)[:, None]
    local_offsets = sep_index.reshape(tile_count, per_share) - bases
    onehot = selector(local_offsets, share_len)
    values = coupled.reshape(rhs_count, tile_count, per_share)
    offsets = local_offsets.astype(jnp.float32)
    got_values, got_offsets = (
        lax.all_to_all(values, "tile", split_axis=1, concat_axis=1, tiled=True),
        lax.all_to_all(offsets[None], "tile", split_axis=1, concat_axis=1, tiled=True),
    )
    got_onehot = selector(got_offsets[0].astype(jnp.int32), share_len)
    own_share = jnp.einsum("rjp,jps->rs", got_values, got_onehot, precision=lax.Precision.HIGHEST)
    own_share = lax.psum(own_share, "grid")
    residue = (rhs_sep.astype(jnp.float32) - own_share).astype(jnp.bfloat16)
    root_part = jnp.dot(residue, root_inv, preferred_element_type=jnp.float32)
    forward_sep = lax.psum(root_part, "tile").astype(jnp.bfloat16)
    solved = lax.dot_general(
        forward_sep, root_inv, (((1,), (1,)), ((), ())), preferred_element_type=jnp.float32
    )
    gathered = lax.all_gather(solved.astype(jnp.bfloat16), "tile", axis=1, tiled=True)
    gathered_split = gathered.astype(jnp.float32).reshape(rhs_count, tile_count, share_len)
    picked = jnp.einsum(
        "rjs,jps->rjp", gathered_split, onehot, precision=lax.Precision.HIGHEST
    ).reshape(rhs_count, coupled_rows)
    weighted = (picked * row_factor[None, :]).astype(jnp.bfloat16)
    update = jnp.dot(weighted, codes, preferred_element_type=jnp.float32)
    misfit = (forward_flat.astype(jnp.float32) - update).astype(jnp.bfloat16)
    results = []
    for block_pos in range(per_dev):
        columns = misfit[:, block_pos * block_len : (block_pos + 1) * block_len]
        results.append(
            lax.dot_general(
                columns,
                diag_inv[block_pos],
                (((1,), (1,)), ((), ())),
                preferred_element_type=jnp.float32,
            )
        )
    result = jnp.concatenate(results, axis=1)
    return (result.astype(jnp.bfloat16), solved)


def solution(mesh):
    return jax.shard_map(
        on_device,
        mesh=mesh,
        in_specs=(
            P(None, ("grid", "tile")),
            P(("grid", "tile"), None, None),
            P(("grid", "tile"), None),
            P(("grid", "tile")),
            P(("grid", "tile")),
            P(("grid", "tile")),
            P(None, "tile"),
            P("tile", None),
        ),
        out_specs=(P(None, ("grid", "tile")), P(None, "tile")),
        check_vma=False,
    )
```

profile of v0, /device:TPU:0, one launch (start us, length us, event | category | flops | bytes accessed | tf_op | source)
XLA Modules:
  0.0 225.6 jit_solution(9238859803063247639)
XLA Ops:
  7.2 0.9 reshape.82
  8.1 0.7 subtract_convert_fusion.2
  8.8 7.3 %all-to-all-start.1 = ((f32[1,8,80]{2,0,1:T(1,128)}), f32[1,8,80]{2,0,1:T(1,128)S(1)}, u32[]{:S(2)}, u32[]{:S(2)}) async-start(f32[1,8,80]{2,0,1:T(1,128)} %subtract_convert_fusion.2), calls=%async_computation.1 | async-start | bytes 8192 | tf_op jit(solution)/shard_map/all_to_all | solution.py:39
  16.0 1.4 convolution_convert_fusion.3
  17.5 1.5 convolution_convert_fusion.4
  19.0 1.5 convolution_convert_fusion.5
  21.1 0.8 convolution_multiply_fusion
  22.0 1.1 copy.15
  23.1 6.1 %all-to-all-start = ((f32[192,8,80]{0,2,1:T(8,128)}), f32[192,8,80]{0,2,1:T(8,128)S(1)}, u32[]{:S(2)}, u32[]{:S(2)}) async-start(f32[192,8,80]{0,2,1:T(8,128)} %bitcast.4), calls=%async_computation | async-start | bytes 1310720 | tf_op jit(solution)/shard_map/all_to_all | solution.py:38
  29.3 16.6 %all-to-all-done = f32[192,8,80]{0,2,1:T(8,128)S(1)} async-done(((f32[192,8,80]{0,2,1:T(8,128)}), f32[192,8,80]{0,2,1:T(8,128)S(1)}, u32[]{:S(2)}, u32[]{:S(2)}) %all-to-all-start) | async-done | bytes 491552 | tf_op jit(solution)/shard_map/all_to_all | solution.py:38
  46.0 1.6 convolution_bitcast_fusion
  47.6 31.3 %all-reduce.3.cloned.1.call-done = f32[192,320]{1,0:T(8,128)} async-done(((f32[192,320]{1,0:T(8,128)}), f32[192,320]{1,0:T(8,128)}) %all-reduce.3.cloned.1.call-update) | async-done | bytes 245776 | tf_op jit(solution)/shard_map/psum | solution.py:43
  79.0 3.5 %fusion.26 = f32[192,2560]{1,0:T(8,128)} fusion(bf16[320,2560]{1,0:T(8,128)(2,1)} %param.15, f32[192,320]{1,0:T(8,128)} %all-reduce.3.cloned.1.call-done, bf16[192,320]{1,0:T(8,128)(2,1)S(1)} %copy-done.2), kind=kOutput, calls=%fused_computation.41 | convolution fusion | flops 314757120 | bytes 3973120 | tf_op jit(solution)/shard_map/dot_general | solution.py:45
  82.5 88.7 %all-reduce.4 = bf16[192,2560]{1,0:T(8,128)(2,1)S(1)} all-reduce(f32[192,2560]{1,0:T(8,128)} %fusion.26), channel_id=1, replica_groups=mesh['grid'=4,'tile'=8] {'tile'}, use_global_device_ids=true, to_apply=%region_1.0 | all-reduce | flops 491520 | bytes 2949120 | tf_op jit(solution)/shard_map/psum | solution.py:46
  171.2 2.2 fusion.29
  173.5 34.6 %all-gather = bf16[8,320,192]{1,2,0:T(8,128)(2,1)S(1)} all-gather(bf16[1,320,192]{1,2,0:T(8,128)(2,1)S(1)} %convert_bitcast_fusion), channel_id=1, replica_groups=mesh['grid'=4,'tile'=8] {'tile'}, dimensions={0}, use_global_device_ids=true | all-gather | bytes 1105920 | tf_op jit(solution)/shard_map/all_gather | solution.py:50
  208.0 0.7 copy.16
  208.7 1.5 reshape.86
  210.3 2.0 reshape.83
  212.3 1.5 fusion.1
  213.8 1.3 copy.18
  215.1 1.8 fusion
  216.9 0.3 convolution_convert_fusion
  217.9 0.9 pad_maximum_fusion.1
  (31 shorter events, 0.9 us)
Async XLA Ops:
  7.2 14.0 %copy-start = (bf16[640,1536]{1,0:T(8,128)(2,1)S(1)}, bf16[640,1536]{1,0:T(8,128)(2,1)}, u32[]{:S(2)}) copy-start(bf16[640,1536]{1,0:T(8,128)(2,1)} %param.10) | copy-start | bytes 5898244
  8.8 14.3 %all-to-all-start.1 = ((f32[1,8,80]{2,0,1:T(1,128)}), f32[1,8,80]{2,0,1:T(1,128)S(1)}, u32[]{:S(2)}, u32[]{:S(2)}) async-start(f32[1,8,80]{2,0,1:T(1,128)} %subtract_convert_fusion.2), calls=%async_computation.1 | async-start | bytes 8192 | tf_op jit(solution)/shard_map/all_to_all | solution.py:39
  16.0 5.1 %copy-start.4 = (f32[640]{0:T(1024)S(1)}, f32[640]{0:T(1024)}, u32[]{:S(2)}) copy-start(f32[640]{0:T(1024)} %param.11) | copy-start | bytes 7684
  17.5 4.5 %copy-start.6 = (bf16[192,512]{1,0:T(8,128)(2,1)}, bf16[192,512]{1,0:T(8,128)(2,1)S(1)}, u32[]{:S(2)}) copy-start(bf16[192,512]{1,0:T(8,128)(2,1)S(1)} %convolution_convert_fusion.3) | copy-start | bytes 589828
  18.9 3.0 %copy-start.8 = (bf16[192,512]{1,0:T(8,128)(2,1)}, bf16[192,512]{1,0:T(8,128)(2,1)S(1)}, u32[]{:S(2)}) copy-start(bf16[192,512]{1,0:T(8,128)(2,1)S(1)} %convolution_convert_fusion.4) | copy-start | bytes 589828
  20.4 1.5 copy-start.9
  22.0 7.3 %copy-start.3 = (s32[640]{0:T(1024)S(1)}, s32[640]{0:T(1024)}, u32[]{:S(2)}) copy-start(s32[640]{0:T(1024)} %param.12) | copy-start | bytes 7684
  23.0 55.9 %copy-start.2 = (bf16[192,320]{1,0:T(8,128)(2,1)S(1)}, bf16[192,320]{1,0:T(8,128)(2,1)}, u32[]{:S(2)}) copy-start(bf16[192,320]{1,0:T(8,128)(2,1)} %param.14) | copy-start | bytes 368644
  23.1 22.9 %all-to-all-start = ((f32[192,8,80]{0,2,1:T(8,128)}), f32[192,8,80]{0,2,1:T(8,128)S(1)}, u32[]{:S(2)}, u32[]{:S(2)}) async-start(f32[192,8,80]{0,2,1:T(8,128)} %bitcast.4), calls=%async_computation | async-start | bytes 1310720 | tf_op jit(solution)/shard_map/all_to_all | solution.py:38
  29.2 49.8 %all-reduce.3.cloned.1.call-start = ((), (), s32[]{:S(2)}) async-start(), calls=%async_computation.2 | async-start | bytes 589824 | tf_op jit(solution)/shard_map/psum | solution.py:43
  173.4 35.3 %copy-start.1 = (f32[192,320]{1,0:T(8,128)}, f32[192,320]{1,0:T(8,128)S(1)}, u32[]{:S(2)}) copy-start(f32[192,320]{1,0:T(8,128)S(1)} %fusion.29) | copy-start | bytes 737284
  212.3 2.8 %copy-start.7 = (bf16[192,512]{1,0:T(8,128)(2,1)S(1)}, bf16[192,512]{1,0:T(8,128)(2,1)}, u32[]{:S(2)}) copy-start(bf16[192,512]{1,0:T(8,128)(2,1)} %copy-done.6) | copy-start | bytes 589828
  215.1 1.8 copy-start.5
Sparse Core Ops, SparseCore 0:
  47.7 31.2 all-reduce.2
where the time goes:
time: 226 us
  blocking collectives  123 us (54%)
  waiting for transfers between devices  48 us (21%)
  matrix products  16.7 us (7%)
  between operations  14.9 us (7%)
  starting transfers between devices  13.4 us (6%)
  local copies, waits for them, and re-layouts  7.63 us (3%)
    psum x1, blocking collectives, on_device(): forward_sep = lax.psum(root_part, 'tile').astype(jnp.bfloat16)  88.7 us
    all_gather x1, blocking collectives, on_device(): lax.all_gather(solved.astype(jnp.bfloat16), 'tile', axis=1, tiled=True)  34.6 us
    psum x1, waiting for transfers between devices, on_device(): own_share = lax.psum(own_share, 'grid')  31.3 us
    all_to_all x1, waiting for transfers between devices, on_device(): lax.all_to_all(values, 'tile', split_axis=1, concat_axis=1, tiled=True)  16.6 us
    all_to_all x1, starting transfers between devices, on_device(): lax.all_to_all(offsets[None], 'tile', split_axis=1, concat_axis=1, tiled=...  7.25 us
    all_to_all x1, starting transfers between devices, on_device(): lax.all_to_all(values, 'tile', split_axis=1, concat_axis=1, tiled=True)  6.13 us
  transfers between devices with their start and end apart: 3, of which 2 were waited for; matrix products, arithmetic and copies ran while one was open for 3% of the time, Pallas kernels for 0%

commit v1 on v0

--- a/solution.py
+++ b/solution.py
@@ -1,8 +1,455 @@
+import functools
+
 import jax
 import jax.numpy as jnp
 from jax import lax
+from jax.experimental import pallas as pl
+from jax.experimental.pallas import tpu as pltpu
 from jax.sharding import PartitionSpec as P
 
+LANES = 128
+ROWS = 16
+MESH = pl.DeviceIdType.MESH
+F32 = jnp.float32
+BF16 = jnp.bfloat16
+NT = (((1,), (1,)), ((), ()))
+
+
+def lane_window(block, width):
+    return block * width // LANES * LANES
+
+
+def kernel(
+    groups,
+    tiles,
+    factor_ref,
+    index_ref,
+    rhs_sep_ref,
+    rhs_hbm,
+    diag_hbm,
+    codes_hbm,
+    root_hbm,
+    out_ref,
+    sep_ref,
+    rhs,
+    diag,
+    codes,
+    root,
+    forward,
+    coupled,
+    index_all,
+    onehot,
+    got,
+    part,
+    part_got,
+    fsep,
+    solved,
+    picked,
+    pick_got,
+    load_sem,
+    code_sem,
+    self_sem,
+    idx_send,
+    idx_recv,
+    a_send,
+    a_recv,
+    r_send,
+    r_recv,
+    f_send,
+    f_recv,
+    s_send,
+    s_recv,
+    b_send,
+    b_recv,
+):
+    g = lax.axis_index("grid")
+    t = lax.axis_index("tile")
+    count = groups * tiles
+    me = g * tiles + t
+    per_dev, block_len = diag.shape[0], diag.shape[1]
+    share = root.shape[0]
+    window = part.shape[2]
+    per_share = codes_hbm.shape[0] // tiles
+    rhs_count = rhs.shape[0]
+    rpg = rhs_count // groups
+    chunk = 2
+    chunks = tiles // chunk
+    wide = chunk * LANES
+
+    def lanes(position, size=LANES):
+        return pl.ds(pl.multiple_of(position * LANES, LANES), size)
+
+    def rows_of(group):
+        return pl.ds(pl.multiple_of(group * rpg, ROWS), rpg)
+
+    barrier = pltpu.get_barrier_semaphore()
+
+    def greet(k, carry):
+        peer = lax.rem(me + k, count)
+        pl.semaphore_signal(
+            barrier, inc=1, device_id=(peer // tiles, lax.rem(peer, tiles)), device_id_type=MESH
+        )
+        return carry
+
+    lax.fori_loop(1, count, greet, 0)
+
+    loads = [pltpu.make_async_copy(rhs_hbm, rhs, load_sem.at[0])]
+    for b in range(per_dev):
+        loads.append(pltpu.make_async_copy(diag_hbm.at[b], diag.at[b], load_sem.at[1 + b]))
+    for load in loads:
+        load.start()
+    code_loads = []
+    for j in range(tiles):
+        code_loads.append(
+            pltpu.make_async_copy(
+                codes_hbm.at[pl.ds(j * per_share, per_share)],
+                codes.at[pl.ds(j * LANES, per_share)],
+                code_sem.at[j],
+            )
+        )
+    for load in code_loads:
+        load.start()
+    root_load = pltpu.make_async_copy(root_hbm, root, load_sem.at[1 + per_dev])
+    root_load.start()
+    if per_share < LANES:
+        for j in range(tiles):
+            codes[j * LANES + per_share : (j + 1) * LANES, :] = jnp.zeros(
+                (LANES - per_share, codes.shape[1]), BF16
+            )
+
+    loads[0].wait()
+    for b in range(per_dev):
+        loads[1 + b].wait()
+        cols = slice(b * block_len, (b + 1) * block_len)
+        forward[:, cols] = jnp.dot(
+            rhs[:, cols], diag[b], preferred_element_type=F32
+        ).astype(BF16)
+
+    pl.semaphore_wait(barrier, count - 1)
+
+    def index_copy(peer, slot, source):
+        return pltpu.make_async_remote_copy(
+            src_ref=index_ref.at[lax.rem(peer, tiles)],
+            dst_ref=index_all.at[slot],
+            send_sem=idx_send.at[peer],
+            recv_sem=idx_recv.at[source],
+            device_id=(peer // tiles, lax.rem(peer, tiles)),
+            device_id_type=MESH,
+        )
+
+    def send_index(k, carry):
+        index_copy(lax.rem(me + k, count), me, me).start()
+        return carry
+
+    lax.fori_loop(1, count, send_index, 0)
+    own_index = pltpu.make_async_copy(index_ref.at[t], index_all.at[me], self_sem.at[0])
+    own_index.start()
+
+    def term_copy(pg, pt, source):
+        return pltpu.make_async_remote_copy(
+            src_ref=coupled.at[rows_of(pg), lanes(pt)],
+            dst_ref=got.at[:, lanes(source)],
+            send_sem=a_send.at[pg * tiles + pt],
+            recv_sem=a_recv.at[source],
+            device_id=(pg, pt),
+            device_id_type=MESH,
+        )
+
+    for load in code_loads:
+        load.wait()
+
+    def couple(i, carry):
+        q = lax.rem(t // chunk + 1 + i, chunks)
+        code_rows = codes[pl.ds(pl.multiple_of(q * wide, wide), wide), :]
+        terms = lax.dot_general(forward[...], code_rows, NT, preferred_element_type=F32)
+        terms = terms * factor_ref[:, pl.ds(pl.multiple_of(q * wide, wide), wide)]
+        coupled[:, pl.ds(pl.multiple_of(q * wide, wide), wide)] = terms.astype(BF16)
+
+        def send(k, inner):
+            pg = lax.rem(g + k // chunk, groups)
+            pt = q * chunk + lax.rem(k, chunk)
+
+            @pl.when(pg * tiles + pt != me)
+            def _():
+                term_copy(pg, pt, me).start()
+
+            return inner
+
+        return lax.fori_loop(0, groups * chunk, send, carry)
+
+    lax.fori_loop(0, chunks, couple, 0)
+    own_terms = pltpu.make_async_copy(
+        coupled.at[rows_of(g), lanes(t)], got.at[:, lanes(me)], self_sem.at[1]
+    )
+    own_terms.start()
+
+    own_index.wait()
+
+    def index_done(k, carry):
+        source = lax.rem(me + k, count)
+        index_copy(source, source, source).wait_recv()
+        return carry
+
+    lax.fori_loop(1, count, index_done, 0)
+
+    def select(source, carry):
+        places = lax.broadcasted_iota(jnp.int32, (share, LANES), 0)
+        onehot[:, lanes(source)] = jnp.where(places == index_all[source], 1.0, 0.0).astype(BF16)
+        return carry
+
+    lax.fori_loop(0, count, select, 0)
+
+    own_terms.wait()
+
+    def terms_done(k, carry):
+        source = lax.rem(me + k, count)
+        term_copy(source // tiles, lax.rem(source, tiles), source).wait_recv()
+        return carry
+
+    lax.fori_loop(1, count, terms_done, 0)
+    own_share = lax.dot_general(got[...], onehot[...], NT, preferred_element_type=F32)
+    residue = (rhs_sep_ref[rows_of(g), :].astype(F32) - own_share).astype(BF16)
+
+    def part_copy(pt, source):
+        return pltpu.make_async_remote_copy(
+            src_ref=part.at[pt],
+            dst_ref=part_got.at[source],
+            send_sem=r_send.at[pt],
+            recv_sem=r_recv.at[source],
+            device_id=(g, pt),
+            device_id_type=MESH,
+        )
+
+    root_load.wait()
+    for c in range(tiles - 1, -1, -1):
+
+        @pl.when(c >= t)
+        def _():
+            first = lane_window(c, share)
+            part[c] = jnp.dot(
+                residue, root[:, first : first + window], preferred_element_type=F32
+            ).astype(BF16)
+
+        @pl.when(c > t)
+        def _():
+            part_copy(c, t).start()
+
+    def add_part(source, total):
+        part_copy(source, source).wait_recv()
+        return total + part_got[source].astype(F32)
+
+    total = lax.fori_loop(0, t, add_part, part[t].astype(F32))
+    offset = t * share - t * share // LANES * LANES
+    column = lax.broadcasted_iota(jnp.int32, (rpg, window), 1)
+    inside = jnp.logical_and(column >= offset, column < offset + share)
+    fsep[t] = jnp.where(inside, total, 0.0).astype(BF16)
+
+    def fsep_copy(pt, source):
+        return pltpu.make_async_remote_copy(
+            src_ref=fsep.at[source],
+            dst_ref=fsep.at[source],
+            send_sem=f_send.at[pt],
+            recv_sem=f_recv.at[source],
+            device_id=(g, pt),
+            device_id_type=MESH,
+        )
+
+    def send_fsep(pt, carry):
+        fsep_copy(pt, t).start()
+        return carry
+
+    lax.fori_loop(0, t, send_fsep, 0)
+    solved[...] = jnp.zeros_like(solved)
+    for c in range(tiles):
+
+        @pl.when(c > t)
+        def _():
+            fsep_copy(c, c).wait_recv()
+
+        @pl.when(c >= t)
+        def _():
+            first = lane_window(c, share)
+            solved[...] += lax.dot_general(
+                fsep[c], root[:, first : first + window], NT, preferred_element_type=F32
+            )
+
+    picked[...] = jnp.dot(
+        solved[...].astype(BF16), onehot[...], preferred_element_type=F32
+    ).astype(BF16)
+
+    def pick_copy(peer, source):
+        return pltpu.make_async_remote_copy(
+            src_ref=picked.at[:, lanes(peer)],
+            dst_ref=pick_got.at[rows_of(source // tiles), lanes(lax.rem(source, tiles))],
+            send_sem=b_send.at[peer],
+            recv_sem=b_recv.at[source],
+            device_id=(peer // tiles, lax.rem(peer, tiles)),
+            device_id_type=MESH,
+        )
+
+    def send_pick(k, carry):
+        pick_copy(lax.rem(me + k, count), me).start()
+        return carry
+
+    lax.fori_loop(1, count, send_pick, 0)
+    own_pick = pltpu.make_async_copy(
+        picked.at[:, lanes(me)], pick_got.at[rows_of(g), lanes(t)], self_sem.at[2]
+    )
+    own_pick.start()
+
+    def sep_copy(pg, source):
+        return pltpu.make_async_remote_copy(
+            src_ref=solved,
+            dst_ref=sep_ref.at[rows_of(source)],
+            send_sem=s_send.at[pg],
+            recv_sem=s_recv.at[source],
+            device_id=(pg, t),
+            device_id_type=MESH,
+        )
+
+    def send_sep(k, carry):
+        sep_copy(lax.rem(g + k, groups), g).start()
+        return carry
+
+    lax.fori_loop(1, groups, send_sep, 0)
+    own_sep = pltpu.make_async_copy(solved, sep_ref.at[rows_of(g)], self_sem.at[3])
+    own_sep.start()
+
+    own_pick.wait()
+
+    def pick_done(k, carry):
+        source = lax.rem(me + k, count)
+        pick_copy(source, source).wait_recv()
+        return carry
+
+    lax.fori_loop(1, count, pick_done, 0)
+    weighted = (pick_got[...].astype(F32) * factor_ref[...]).astype(BF16)
+    for b in range(per_dev):
+        cols = slice(b * block_len, (b + 1) * block_len)
+        update = jnp.dot(weighted, codes[:, cols], preferred_element_type=F32)
+        misfit = (forward[:, cols].astype(F32) - update).astype(BF16)
+        out_ref[:, cols] = lax.dot_general(
+            misfit, diag[b], NT, preferred_element_type=F32
+        ).astype(BF16)
+
+    own_sep.wait()
+
+    def sep_done(k, carry):
+        source = lax.rem(g + k, groups)
+        sep_copy(source, source).wait_recv()
+        sep_copy(source, g).wait_send()
+        return carry
+
+    lax.fori_loop(1, groups, sep_done, 0)
+
+    def sent(k, carry):
+        peer = lax.rem(me + k, count)
+        index_copy(peer, me, me).wait_send()
+        term_copy(peer // tiles, lax.rem(peer, tiles), me).wait_send()
+        pick_copy(peer, me).wait_send()
+        return carry
+
+    lax.fori_loop(1, count, sent, 0)
+
+    def part_sent(pt, carry):
+        part_copy(pt, t).wait_send()
+        return carry
+
+    lax.fori_loop(t + 1, tiles, part_sent, 0)
+
+    def fsep_sent(pt, carry):
+        fsep_copy(pt, t).wait_send()
+        return carry
+
+    lax.fori_loop(0, t, fsep_sent, 0)
+
+
+def fused(rhs_local, diag_inv, codes, row_scales, sep_index, live_rows, rhs_sep, root_inv):
+    rhs_count, local_len = rhs_local.shape
+    per_dev, block_len = diag_inv.shape[0], diag_inv.shape[1]
+    coupled_rows = codes.shape[0]
+    share, sep_len = root_inv.shape
+    groups, tiles = lax.axis_size("grid"), lax.axis_size("tile")
+    count = groups * tiles
+    per_share = coupled_rows // tiles
+    rpg = rhs_count // groups
+    window = share + (-share) % LANES
+    pad = ((0, 0), (0, LANES - per_share))
+    positions = jnp.arange(coupled_rows, dtype=jnp.int32)
+    factor = row_scales * (positions < live_rows[0]).astype(F32)
+    factor = jnp.pad(factor.reshape(tiles, per_share), pad).reshape(1, tiles * LANES)
+    bases = (jnp.arange(tiles, dtype=jnp.int32) * share)[:, None]
+    index = jnp.pad(
+        sep_index.reshape(tiles, per_share) - bases, pad, constant_values=-1
+    ).reshape(tiles, 1, LANES)
+    vmem = pl.BlockSpec(memory_space=pltpu.VMEM)
+    anywhere = pl.BlockSpec(memory_space=pl.ANY)
+    dma = pltpu.SemaphoreType.DMA
+    macs = rhs_count * local_len * 2 * (block_len + tiles * LANES)
+    return pl.pallas_call(
+        functools.partial(kernel, groups, tiles),
+        out_shape=(
+            jax.ShapeDtypeStruct((rhs_count, local_len), BF16),
+            jax.ShapeDtypeStruct((rhs_count, share), F32),
+        ),
+        in_specs=[vmem, vmem, vmem, anywhere, anywhere, anywhere, anywhere],
+        out_specs=(vmem, vmem),
+        scratch_shapes=[
+            pltpu.VMEM((rhs_count, local_len), BF16),
+            pltpu.VMEM(diag_inv.shape, BF16),
+            pltpu.VMEM((tiles * LANES, local_len), BF16),
+            pltpu.VMEM(root_inv.shape, BF16),
+            pltpu.VMEM((rhs_count, local_len), BF16),
+            pltpu.VMEM((rhs_count, tiles * LANES), BF16),
+            pltpu.VMEM((count, 1, LANES), jnp.int32),
+            pltpu.VMEM((share, count * LANES), BF16),
+            pltpu.VMEM((rpg, count * LANES), BF16),
+            pltpu.VMEM((tiles, rpg, window), BF16),
+            pltpu.VMEM((tiles, rpg, window), BF16),
+            pltpu.VMEM((tiles, rpg, window), BF16),
+            pltpu.VMEM((rpg, share), F32),
+            pltpu.VMEM((rpg, count * LANES), BF16),
+            pltpu.VMEM((rhs_count, tiles * LANES), BF16),
+            dma((2 + per_dev,)),
+            dma((tiles,)),
+            dma((4,)),
+            dma((count,)),
+            dma((count,)),
+            dma((count,)),
+            dma((count,)),
+            dma((tiles,)),
+            dma((tiles,)),
+            dma((tiles,)),
+            dma((tiles,)),
+            dma((groups,)),
+            dma((groups,)),
+            dma((count,)),
+            dma((count,)),
+        ],
+        compiler_params=pltpu.CompilerParams(
+            collective_id=0, has_side_effects=True, vmem_limit_bytes=48 * 1024 * 1024
+        ),
+        cost_estimate=pl.CostEstimate(
+            flops=2 * macs,
+            bytes_accessed=2 * (diag_inv.size + codes.size + root_inv.size + 2 * rhs_local.size),
+            transcendentals=0,
+        ),
+    )(factor, index, rhs_sep, rhs_local, diag_inv, codes, root_inv)
+
+
+def fits(mesh, rhs_local, diag_inv, codes, root_inv):
+    groups, tiles = mesh.shape["grid"], mesh.shape["tile"]
+    rhs_count = rhs_local.shape[0]
+    per_share = codes.shape[0] // (groups * tiles) // tiles
+    share = root_inv.shape[0] // tiles
+    return (
+        rhs_count % (groups * ROWS) == 0
+        and tiles % 2 == 0
+        and per_share % ROWS == 0
+        and per_share <= LANES
+        and share % (LANES // 2) == 0
+        and diag_inv.shape[1] % LANES == 0
+    )
 
 def selector(offsets, share_len):
     columns = jnp.arange(share_len, dtype=jnp.int32)
@@ -71,19 +518,26 @@
 
 
 def solution(mesh):
-    return jax.shard_map(
-        on_device,
-        mesh=mesh,
-        in_specs=(
-            P(None, ("grid", "tile")),
-            P(("grid", "tile"), None, None),
-            P(("grid", "tile"), None),
-            P(("grid", "tile")),
-            P(("grid", "tile")),
-            P(("grid", "tile")),
-            P(None, "tile"),
-            P("tile", None),
-        ),
-        out_specs=(P(None, ("grid", "tile")), P(None, "tile")),
-        check_vma=False,
-    )
+    specs = (
+        P(None, ("grid", "tile")),
+        P(("grid", "tile"), None, None),
+        P(("grid", "tile"), None),
+        P(("grid", "tile")),
+        P(("grid", "tile")),
+        P(("grid", "tile")),
+        P(None, "tile"),
+        P("tile", None),
+    )
+
+    def run(*args):
+        rhs_local, diag_inv, codes, root_inv = args[0], args[1], args[2], args[7]
+        body = fused if fits(mesh, rhs_local, diag_inv, codes, root_inv) else on_device
+        return jax.shard_map(
+            body,
+            mesh=mesh,
+            in_specs=specs,
+            out_specs=(P(None, ("grid", "tile")), P(None, "tile")),
+            check_vma=False,
+        )(*args)
+
+    return run

time: 226 us -> 59.6 us (0.26)
  the two profiles are of different devices: /device:TPU:0 before, /device:TPU:25 now
where the time goes in v1:
time: 59.6 us; the launch traced here: 59.3 us
  Pallas kernels  50.1 us (84%)
  local copies, waits for them, and re-layouts  7.2 us (12%)
  between operations  1.3 us (2%)
  other arithmetic  0.77 us (1%)
    pallas_call x1, Pallas kernels, fused(): pl.pallas_call(functools.partial(kernel, groups, tiles), out_shape=(jax.S...  50.1 us
    unnamed x10, local copies, waits for them, and re-layouts  6.34 us

profile of v1, /device:TPU:25, one launch (start us, length us, event | category | flops | bytes accessed | tf_op | source)
XLA Modules:
  0.0 59.3 jit_solution(2364500561219091927)
XLA Ops:
  1.3 0.7 %fusion = f32[640]{0:T(1024)S(1)} fusion(f32[640]{0:T(1024)} %param.11, s32[]{:T(128)} %bitcast.3), kind=kLoop, calls=%fused_computation.1 | loop fusion | flops 1280 | bytes 5124 | tf_op jit(solution)/shard_map/mul | solution.py:379
  2.0 0.1 reshape.20
  2.1 0.8 %reshape.22 = s32[8,80]{1,0:T(8,128)S(1)} reshape(s32[640]{0:T(1024)} %param.12) | data formatting | bytes 5120 | tf_op jit(solution)/shard_map/reshape | solution.py:383
  2.8 0.1 broadcast_subtract_fusion
  2.9 0.0 copy-start
  2.9 1.4 %copy-done = bf16[320,2560]{1,0:T(8,128)(2,1)S(1)} copy-done((bf16[320,2560]{1,0:T(8,128)(2,1)S(1)}, bf16[320,2560]{1,0:T(8,128)(2,1)}, u32[]{:S(2)}) %copy-start) | copy-done | bytes 1638424
  4.3 0.0 copy-start.1
  4.3 1.4 %copy-done.1 = bf16[3,512,512]{2,1,0:T(8,128)(2,1)S(1)} copy-done((bf16[3,512,512]{2,1,0:T(8,128)(2,1)S(1)}, bf16[3,512,512]{2,1,0:T(8,128)(2,1)}, u32[]{:S(2)}) %copy-start.1) | copy-done | bytes 1572888
  5.8 0.0 copy-start.2
  5.8 1.1 %copy-done.2 = bf16[192,1536]{1,0:T(8,128)(2,1)S(1)} copy-done((bf16[192,1536]{1,0:T(8,128)(2,1)S(1)}, bf16[192,1536]{1,0:T(8,128)(2,1)}, u32[]{:S(2)}) %copy-start.2) | copy-done | bytes 589848
  6.8 0.0 copy-start.3
  6.8 0.9 %copy-done.3 = bf16[192,320]{1,0:T(8,128)(2,1)S(1)} copy-done((bf16[192,320]{1,0:T(8,128)(2,1)S(1)}, bf16[192,320]{1,0:T(8,128)(2,1)}, u32[]{:S(2)}) %copy-start.3) | copy-done | bytes 122904
  7.7 50.1 %shard_map.95 = (bf16[192,1536]{1,0:T(8,128)(2,1)S(1)}, f32[192,320]{1,0:T(8,128)S(1)}) custom-call(f32[1,1024]{1,0:T(1,128)S(1)} %bitcast.4, s32[8,1,128]{2,1,0:T(1,128)S(1)} %bitcast.5, bf16[192,320]{1,0:T(8,128)(2,1)S(1)} %copy-done.3, bf16[192,1536]{1,0:T(8,128)(2,1)S(1)} %copy-done.2, bf16[3,512,512]{2,1,0:T(8,128)(2,1)S(1)} %copy-done.1, ...), custom_call_target="tpu_custom_call" | custom-call | flops 1811939328 | bytes 6356992 | tf_op jit(solution)/shard_map/pallas_call | solution.py:389
  57.8 0.8 %copy.13 = bf16[192,1536]{1,0:T(8,128)(2,1)} copy(bf16[192,1536]{1,0:T(8,128)(2,1)S(1)} %get-tuple-element.4) | data formatting | bytes 1179648
  58.6 0.7 %copy.14 = f32[192,320]{1,0:T(8,128)} copy(f32[192,320]{1,0:T(8,128)S(1)} %get-tuple-element.5) | data formatting | bytes 491520
  (3 shorter events, 0.0 us)
Async XLA Ops:
  2.9 1.4 %copy-start = (bf16[320,2560]{1,0:T(8,128)(2,1)S(1)}, bf16[320,2560]{1,0:T(8,128)(2,1)}, u32[]{:S(2)}) copy-start(bf16[320,2560]{1,0:T(8,128)(2,1)} %root_hbm.1) | copy-start | bytes 4915204
  4.3 1.4 %copy-start.1 = (bf16[3,512,512]{2,1,0:T(8,128)(2,1)S(1)}, bf16[3,512,512]{2,1,0:T(8,128)(2,1)}, u32[]{:S(2)}) copy-start(bf16[3,512,512]{2,1,0:T(8,128)(2,1)} %diag_hbm.1) | copy-start | bytes 4718596
  5.8 1.1 %copy-start.2 = (bf16[192,1536]{1,0:T(8,128)(2,1)S(1)}, bf16[192,1536]{1,0:T(8,128)(2,1)}, u32[]{:S(2)}) copy-start(bf16[192,1536]{1,0:T(8,128)(2,1)} %rhs_hbm.1) | copy-start | bytes 1769476
  6.8 0.9 %copy-start.3 = (bf16[192,320]{1,0:T(8,128)(2,1)S(1)}, bf16[192,320]{1,0:T(8,128)(2,1)}, u32[]{:S(2)}) copy-start(bf16[192,320]{1,0:T(8,128)(2,1)} %rhs_sep_ref.1) | copy-start | bytes 368644

commit v2 on v1

--- a/solution.py
+++ b/solution.py
@@ -15,8 +15,41 @@
 NT = (((1,), (1,)), ((), ()))
 
 
-def lane_window(block, width):
-    return block * width // LANES * LANES
+def lane_index(rows):
+    return lax.broadcasted_iota(jnp.int32, (rows, LANES), 1)
+
+
+def pack(pieces, length):
+    tiles = [None] * pl.cdiv(len(pieces) * length, LANES)
+    lane = lane_index(pieces[0].shape[0])
+
+    def add(tile, piece):
+        tiles[tile] = piece if tiles[tile] is None else tiles[tile] + piece
+
+    for pos, piece in enumerate(pieces):
+        tile, shift = pos * length // LANES, pos * length % LANES
+        turned = pltpu.roll(piece, shift, 1) if shift else piece
+        if shift + length > LANES:
+            add(tile, jnp.where(lane >= shift, turned, 0.0))
+            add(tile + 1, jnp.where(lane < shift, turned, 0.0))
+        else:
+            add(tile, turned)
+    return jnp.concatenate(tiles, axis=1)
+
+
+def unpack(packed, pieces, length):
+    lane = lane_index(packed.shape[0])
+    out = []
+    for pos in range(pieces):
+        tile, shift = pos * length // LANES, pos * length % LANES
+        piece = packed[:, tile * LANES : (tile + 1) * LANES]
+        if shift:
+            piece = pltpu.roll(piece, LANES - shift, 1)
+        if shift + length > LANES:
+            rest = packed[:, (tile + 1) * LANES : (tile + 2) * LANES]
+            piece = jnp.where(lane < LANES - shift, piece, pltpu.roll(rest, LANES - shift, 1))
+        out.append(piece)
+    return out
 
 
 def kernel(
@@ -43,9 +76,11 @@
     part,
     part_got,
     fsep,
+    total,
     solved,
     picked,
     pick_got,
+    update,
     load_sem,
     code_sem,
     self_sem,
@@ -65,29 +100,37 @@
     g = lax.axis_index("grid")
     t = lax.axis_index("tile")
     count = groups * tiles
-    me = g * tiles + t
+    mine = t * groups + g
     per_dev, block_len = diag.shape[0], diag.shape[1]
     share = root.shape[0]
-    window = part.shape[2]
     per_share = codes_hbm.shape[0] // tiles
     rhs_count = rhs.shape[0]
     rpg = rhs_count // groups
-    chunk = 2
-    chunks = tiles // chunk
-    wide = chunk * LANES
+    subs = rpg // ROWS
+    span = groups * ROWS
+    pairs = tiles // 2
+    wide = 2 * LANES
+    fan = 2 * groups
+    pair_me = t // 2
+    toward = 1 - 2 * (2 * pair_me // pairs)
+
+    def pair_at(distance):
+        return lax.rem(pair_me + toward * distance + pairs, pairs)
 
     def lanes(position, size=LANES):
-        return pl.ds(pl.multiple_of(position * LANES, LANES), size)
+        return pl.ds(pl.multiple_of(position * size, size), size)
 
     def rows_of(group):
-        return pl.ds(pl.multiple_of(group * rpg, ROWS), rpg)
+        return pl.ds(pl.multiple_of(group * ROWS, ROWS), ROWS)
+
+    def device(slot):
+        return (lax.rem(slot, groups), slot // groups)
 
     barrier = pltpu.get_barrier_semaphore()
 
     def greet(k, carry):
-        peer = lax.rem(me + k, count)
         pl.semaphore_signal(
-            barrier, inc=1, device_id=(peer // tiles, lax.rem(peer, tiles)), device_id_type=MESH
+            barrier, inc=1, device_id=device(lax.rem(mine + k, count)), device_id_type=MESH
         )
         return carry
 
@@ -127,31 +170,31 @@
 
     pl.semaphore_wait(barrier, count - 1)
 
-    def index_copy(peer, slot, source):
+    def index_copy(peer, source):
         return pltpu.make_async_remote_copy(
-            src_ref=index_ref.at[lax.rem(peer, tiles)],
-            dst_ref=index_all.at[slot],
+            src_ref=index_ref.at[peer // groups],
+            dst_ref=index_all.at[source],
             send_sem=idx_send.at[peer],
             recv_sem=idx_recv.at[source],
-            device_id=(peer // tiles, lax.rem(peer, tiles)),
+            device_id=device(peer),
             device_id_type=MESH,
         )
 
     def send_index(k, carry):
-        index_copy(lax.rem(me + k, count), me, me).start()
+        index_copy(lax.rem(mine + k, count), mine).start()
         return carry
 
     lax.fori_loop(1, count, send_index, 0)
-    own_index = pltpu.make_async_copy(index_ref.at[t], index_all.at[me], self_sem.at[0])
+    own_index = pltpu.make_async_copy(index_ref.at[t], index_all.at[mine], self_sem.at[0])
     own_index.start()
 
-    def term_copy(pg, pt, source):
+    def term_copy(peer, source):
         return pltpu.make_async_remote_copy(
-            src_ref=coupled.at[rows_of(pg), lanes(pt)],
-            dst_ref=got.at[:, lanes(source)],
-            send_sem=a_send.at[pg * tiles + pt],
+            src_ref=coupled.at[peer // groups, rows_of(lax.rem(peer, groups))],
+            dst_ref=got.at[source],
+            send_sem=a_send.at[peer],
             recv_sem=a_recv.at[source],
-            device_id=(pg, pt),
+            device_id=device(peer),
             device_id_type=MESH,
         )
 
@@ -159,35 +202,36 @@
         load.wait()
 
     def couple(i, carry):
-        q = lax.rem(t // chunk + 1 + i, chunks)
-        code_rows = codes[pl.ds(pl.multiple_of(q * wide, wide), wide), :]
-        terms = lax.dot_general(forward[...], code_rows, NT, preferred_element_type=F32)
-        terms = terms * factor_ref[:, pl.ds(pl.multiple_of(q * wide, wide), wide)]
-        coupled[:, pl.ds(pl.multiple_of(q * wide, wide), wide)] = terms.astype(BF16)
+        q = pair_at(pairs - 1 - i)
+        terms = lax.dot_general(
+            forward[...], codes[lanes(q, wide), :], NT, preferred_element_type=F32
+        )
+        terms = terms * factor_ref[:, lanes(q, wide)]
+        for u in range(2):
+            ours = terms[:, u * LANES : (u + 1) * LANES]
+            pieces = [ours[j * span : (j + 1) * span] for j in range(subs)]
+            coupled[2 * q + u] = pack(pieces, per_share).astype(BF16)
 
         def send(k, inner):
-            pg = lax.rem(g + k // chunk, groups)
-            pt = q * chunk + lax.rem(k, chunk)
-
-            @pl.when(pg * tiles + pt != me)
+            peer = q * fan + k
+
+            @pl.when(peer != mine)
             def _():
-                term_copy(pg, pt, me).start()
+                term_copy(peer, mine).start()
 
             return inner
 
-        return lax.fori_loop(0, groups * chunk, send, carry)
-
-    lax.fori_loop(0, chunks, couple, 0)
-    own_terms = pltpu.make_async_copy(
-        coupled.at[rows_of(g), lanes(t)], got.at[:, lanes(me)], self_sem.at[1]
-    )
+        return lax.fori_loop(0, fan, send, carry)
+
+    lax.fori_loop(0, pairs, couple, 0)
+    own_terms = pltpu.make_async_copy(coupled.at[t, rows_of(g)], got.at[mine], self_sem.at[1])
     own_terms.start()
 
     own_index.wait()
 
     def index_done(k, carry):
-        source = lax.rem(me + k, count)
-        index_copy(source, source, source).wait_recv()
+        source = lax.rem(mine + k, count)
+        index_copy(source, source).wait_recv()
         return carry
 
     lax.fori_loop(1, count, index_done, 0)
@@ -200,107 +244,154 @@
     lax.fori_loop(0, count, select, 0)
 
     own_terms.wait()
-
-    def terms_done(k, carry):
-        source = lax.rem(me + k, count)
-        term_copy(source // tiles, lax.rem(source, tiles), source).wait_recv()
-        return carry
-
-    lax.fori_loop(1, count, terms_done, 0)
-    own_share = lax.dot_general(got[...], onehot[...], NT, preferred_element_type=F32)
-    residue = (rhs_sep_ref[rows_of(g), :].astype(F32) - own_share).astype(BF16)
-
-    def part_copy(pt, source):
+    total[...] = jnp.zeros_like(total)
+
+    def gather_terms(i, carry):
+        q = pair_at(i)
+
+        def arrived(k, inner):
+            source = q * fan + k
+
+            @pl.when(source != mine)
+            def _():
+                term_copy(source, source).wait_recv()
+
+            return inner
+
+        lax.fori_loop(0, fan, arrived, 0)
+        columns = []
+        for k in range(fan):
+            pieces = unpack(got[q * fan + k].astype(F32), subs, per_share)
+            columns.append(jnp.concatenate(pieces, axis=0).astype(BF16))
+        total[...] += lax.dot_general(
+            jnp.concatenate(columns, axis=1),
+            onehot[:, lanes(q, fan * LANES)],
+            NT,
+            preferred_element_type=F32,
+        )
+        return carry
+
+    lax.fori_loop(0, pairs, gather_terms, 0)
+    rhs_sep = jnp.concatenate(
+        [
+            rhs_sep_ref[pl.ds(pl.multiple_of(j * span + g * ROWS, ROWS), ROWS), :]
+            for j in range(subs)
+        ],
+        axis=0,
+    )
+    residue = (rhs_sep.astype(F32) - total[...]).astype(BF16)
+
+    def owner_of(pair):
+        return max(pair - 1, 0) * 2 + lax.rem(g, 2)
+
+    def part_copy(pair, source):
         return pltpu.make_async_remote_copy(
-            src_ref=part.at[pt],
-            dst_ref=part_got.at[source],
-            send_sem=r_send.at[pt],
-            recv_sem=r_recv.at[source],
-            device_id=(g, pt),
+            src_ref=part.at[pair],
+            dst_ref=part_got.at[pair, source],
+            send_sem=r_send.at[pair],
+            recv_sem=r_recv.at[pair, source],
+            device_id=(g, owner_of(pair)),
             device_id_type=MESH,
         )
 
+    def block(pair):
+        return slice(pair * 2 * share, (pair + 1) * 2 * share)
+
     root_load.wait()
-    for c in range(tiles - 1, -1, -1):
-
-        @pl.when(c >= t)
+    for pair in range(pairs - 1, -1, -1):
+
+        @pl.when(t < 2 * pair + 2)
         def _():
-            first = lane_window(c, share)
-            part[c] = jnp.dot(
-                residue, root[:, first : first + window], preferred_element_type=F32
+            part[pair] = jnp.dot(
+                residue, root[:, block(pair)], preferred_element_type=F32
             ).astype(BF16)
 
-        @pl.when(c > t)
+            @pl.when(t != owner_of(pair))
+            def _():
+                part_copy(pair, t).start()
+
+    def fsep_copy(pair, peer):
+        return pltpu.make_async_remote_copy(
+            src_ref=fsep.at[pair],
+            dst_ref=fsep.at[pair],
+            send_sem=f_send.at[pair, peer],
+            recv_sem=f_recv.at[pair],
+            device_id=(g, peer),
+            device_id_type=MESH,
+        )
+
+    for pair in range(pairs):
+
+        @pl.when(t == owner_of(pair))
         def _():
-            part_copy(c, t).start()
-
-    def add_part(source, total):
-        part_copy(source, source).wait_recv()
-        return total + part_got[source].astype(F32)
-
-    total = lax.fori_loop(0, t, add_part, part[t].astype(F32))
-    offset = t * share - t * share // LANES * LANES
-    column = lax.broadcasted_iota(jnp.int32, (rpg, window), 1)
-    inside = jnp.logical_and(column >= offset, column < offset + share)
-    fsep[t] = jnp.where(inside, total, 0.0).astype(BF16)
-
-    def fsep_copy(pt, source):
-        return pltpu.make_async_remote_copy(
-            src_ref=fsep.at[source],
-            dst_ref=fsep.at[source],
-            send_sem=f_send.at[pt],
-            recv_sem=f_recv.at[source],
-            device_id=(g, pt),
-            device_id_type=MESH,
-        )
-
-    def send_fsep(pt, carry):
-        fsep_copy(pt, t).start()
-        return carry
-
-    lax.fori_loop(0, t, send_fsep, 0)
-    solved[...] = jnp.zeros_like(solved)
-    for c in range(tiles):
-
-        @pl.when(c > t)
+            def add_part(k, summed):
+                source = lax.rem(t + k, 2 * pair + 2)
+                part_copy(pair, source).wait_recv()
+                return summed + part_got[pair, source].astype(F32)
+
+            summed = lax.fori_loop(1, 2 * pair + 2, add_part, part[pair].astype(F32))
+            fsep[pair] = summed.astype(BF16)
+
+            def send_fsep(k, carry):
+                fsep_copy(pair, lax.rem(t + k, 2 * pair + 2)).start()
+                return carry
+
+            lax.fori_loop(1, 2 * pair + 2, send_fsep, 0)
+
+    total[...] = jnp.zeros_like(total)
+    for pair in range(pairs):
+
+        @pl.when(t < 2 * pair + 2)
         def _():
-            fsep_copy(c, c).wait_recv()
-
-        @pl.when(c >= t)
-        def _():
-            first = lane_window(c, share)
-            solved[...] += lax.dot_general(
-                fsep[c], root[:, first : first + window], NT, preferred_element_type=F32
+            @pl.when(t != owner_of(pair))
+            def _():
+                fsep_copy(pair, t).wait_recv()
+
+            total[...] += lax.dot_general(
+                fsep[pair], root[:, block(pair)], NT, preferred_element_type=F32
             )
 
-    picked[...] = jnp.dot(
-        solved[...].astype(BF16), onehot[...], preferred_element_type=F32
-    ).astype(BF16)
+    for j in range(subs):
+        solved[j] = total[j * ROWS : (j + 1) * ROWS, :]
+    rounded = total[...].astype(BF16)
 
     def pick_copy(peer, source):
         return pltpu.make_async_remote_copy(
-            src_ref=picked.at[:, lanes(peer)],
-            dst_ref=pick_got.at[rows_of(source // tiles), lanes(lax.rem(source, tiles))],
+            src_ref=picked.at[peer],
+            dst_ref=pick_got.at[source // groups, rows_of(lax.rem(source, groups))],
             send_sem=b_send.at[peer],
             recv_sem=b_recv.at[source],
-            device_id=(peer // tiles, lax.rem(peer, tiles)),
+            device_id=device(peer),
             device_id_type=MESH,
         )
 
-    def send_pick(k, carry):
-        pick_copy(lax.rem(me + k, count), me).start()
-        return carry
-
-    lax.fori_loop(1, count, send_pick, 0)
-    own_pick = pltpu.make_async_copy(
-        picked.at[:, lanes(me)], pick_got.at[rows_of(g), lanes(t)], self_sem.at[2]
-    )
+    def pick(i, carry):
+        q = pair_at(pairs - 1 - i)
+        found = jnp.dot(rounded, onehot[:, lanes(q, fan * LANES)], preferred_element_type=F32)
+        for k in range(fan):
+            ours = found[:, k * LANES : (k + 1) * LANES]
+            pieces = [ours[j * ROWS : (j + 1) * ROWS] for j in range(subs)]
+            picked[q * fan + k] = pack(pieces, per_share).astype(BF16)
+
+        def send(k, inner):
+            peer = q * fan + k
+
+            @pl.when(peer != mine)
+            def _():
+                pick_copy(peer, mine).start()
+
+            return inner
+
+        return lax.fori_loop(0, fan, send, carry)
+
+    lax.fori_loop(0, pairs, pick, 0)
+    own_pick = pltpu.make_async_copy(picked.at[mine], pick_got.at[t, rows_of(g)], self_sem.at[2])
     own_pick.start()
 
     def sep_copy(pg, source):
         return pltpu.make_async_remote_copy(
             src_ref=solved,
-            dst_ref=sep_ref.at[rows_of(source)],
+            dst_ref=sep_ref.at[:, rows_of(source)],
             send_sem=s_send.at[pg],
             recv_sem=s_recv.at[source],
             device_id=(pg, t),
@@ -312,22 +403,39 @@
         return carry
 
     lax.fori_loop(1, groups, send_sep, 0)
-    own_sep = pltpu.make_async_copy(solved, sep_ref.at[rows_of(g)], self_sem.at[3])
+    own_sep = pltpu.make_async_copy(solved, sep_ref.at[:, rows_of(g)], self_sem.at[3])
     own_sep.start()
 
     own_pick.wait()
-
-    def pick_done(k, carry):
-        source = lax.rem(me + k, count)
-        pick_copy(source, source).wait_recv()
-        return carry
-
-    lax.fori_loop(1, count, pick_done, 0)
-    weighted = (pick_got[...].astype(F32) * factor_ref[...]).astype(BF16)
+    update[...] = jnp.zeros_like(update)
+
+    def gather_picks(i, carry):
+        q = pair_at(i)
+
+        def arrived(k, inner):
+            source = q * fan + k
+
+            @pl.when(source != mine)
+            def _():
+                pick_copy(source, source).wait_recv()
+
+            return inner
+
+        lax.fori_loop(0, fan, arrived, 0)
+        columns = []
+        for u in range(2):
+            pieces = unpack(pick_got[2 * q + u].astype(F32), subs, per_share)
+            columns.append(jnp.concatenate(pieces, axis=0))
+        weighted = jnp.concatenate(columns, axis=1) * factor_ref[:, lanes(q, wide)]
+        update[...] += jnp.dot(
+            weighted.astype(BF16), codes[lanes(q, wide), :], preferred_element_type=F32
+        )
+        return carry
+
+    lax.fori_loop(0, pairs, gather_picks, 0)
     for b in range(per_dev):
         cols = slice(b * block_len, (b + 1) * block_len)
-        update = jnp.dot(weighted, codes[:, cols], preferred_element_type=F32)
-        misfit = (forward[:, cols].astype(F32) - update).astype(BF16)
+        misfit = (forward[:, cols].astype(F32) - update[:, cols]).astype(BF16)
         out_ref[:, cols] = lax.dot_general(
             misfit, diag[b], NT, preferred_element_type=F32
         ).astype(BF16)
@@ -343,25 +451,26 @@
     lax.fori_loop(1, groups, sep_done, 0)
 
     def sent(k, carry):
-        peer = lax.rem(me + k, count)
-        index_copy(peer, me, me).wait_send()
-        term_copy(peer // tiles, lax.rem(peer, tiles), me).wait_send()
-        pick_copy(peer, me).wait_send()
+        peer = lax.rem(mine + k, count)
+        index_copy(peer, mine).wait_send()
+        term_copy(peer, mine).wait_send()
+        pick_copy(peer, mine).wait_send()
         return carry
 
     lax.fori_loop(1, count, sent, 0)
-
-    def part_sent(pt, carry):
-        part_copy(pt, t).wait_send()
-        return carry
-
-    lax.fori_loop(t + 1, tiles, part_sent, 0)
-
-    def fsep_sent(pt, carry):
-        fsep_copy(pt, t).wait_send()
-        return carry
-
-    lax.fori_loop(0, t, fsep_sent, 0)
+    for pair in range(pairs):
+
+        @pl.when(jnp.logical_and(t < 2 * pair + 2, t != owner_of(pair)))
+        def _():
+            part_copy(pair, t).wait_send()
+
+        @pl.when(t == owner_of(pair))
+        def _():
+            def fsep_sent(k, carry):
+                fsep_copy(pair, lax.rem(t + k, 2 * pair + 2)).wait_send()
+                return carry
+
+            lax.fori_loop(1, 2 * pair + 2, fsep_sent, 0)
 
 
 def fused(rhs_local, diag_inv, codes, row_scales, sep_index, live_rows, rhs_sep, root_inv):
@@ -373,7 +482,8 @@
     count = groups * tiles
     per_share = coupled_rows // tiles
     rpg = rhs_count // groups
-    window = share + (-share) % LANES
+    subs, pairs = rpg // ROWS, tiles // 2
+    packed = pl.cdiv(subs * per_share, LANES) * LANES
     pad = ((0, 0), (0, LANES - per_share))
     positions = jnp.arange(coupled_rows, dtype=jnp.int32)
     factor = row_scales * (positions < live_rows[0]).astype(F32)
@@ -386,11 +496,11 @@
     anywhere = pl.BlockSpec(memory_space=pl.ANY)
     dma = pltpu.SemaphoreType.DMA
     macs = rhs_count * local_len * 2 * (block_len + tiles * LANES)
-    return pl.pallas_call(
+    local, sep = pl.pallas_call(
         functools.partial(kernel, groups, tiles),
         out_shape=(
             jax.ShapeDtypeStruct((rhs_count, local_len), BF16),
-            jax.ShapeDtypeStruct((rhs_count, share), F32),
+            jax.ShapeDtypeStruct((subs, groups * ROWS, share), F32),
         ),
         in_specs=[vmem, vmem, vmem, anywhere, anywhere, anywhere, anywhere],
         out_specs=(vmem, vmem),
@@ -400,16 +510,18 @@
             pltpu.VMEM((tiles * LANES, local_len), BF16),
             pltpu.VMEM(root_inv.shape, BF16),
             pltpu.VMEM((rhs_count, local_len), BF16),
-            pltpu.VMEM((rhs_count, tiles * LANES), BF16),
+            pltpu.VMEM((tiles, groups * ROWS, packed), BF16),
             pltpu.VMEM((count, 1, LANES), jnp.int32),
             pltpu.VMEM((share, count * LANES), BF16),
-            pltpu.VMEM((rpg, count * LANES), BF16),
-            pltpu.VMEM((tiles, rpg, window), BF16),
-            pltpu.VMEM((tiles, rpg, window), BF16),
-            pltpu.VMEM((tiles, rpg, window), BF16),
+            pltpu.VMEM((count, ROWS, packed), BF16),
+            pltpu.VMEM((pairs, rpg, 2 * share), BF16),
+            pltpu.VMEM((pairs, tiles, rpg, 2 * share), BF16),
+            pltpu.VMEM((pairs, rpg, 2 * share), BF16),
             pltpu.VMEM((rpg, share), F32),
-            pltpu.VMEM((rpg, count * LANES), BF16),
-            pltpu.VMEM((rhs_count, tiles * LANES), BF16),
+            pltpu.VMEM((subs, ROWS, share), F32),
+            pltpu.VMEM((count, ROWS, packed), BF16),
+            pltpu.VMEM((tiles, groups * ROWS, packed), BF16),
+            pltpu.VMEM((rhs_count, local_len), F32),
             dma((2 + per_dev,)),
             dma((tiles,)),
             dma((4,)),
@@ -417,17 +529,17 @@
             dma((count,)),
             dma((count,)),
             dma((count,)),
-            dma((tiles,)),
-            dma((tiles,)),
-            dma((tiles,)),
-            dma((tiles,)),
+            dma((pairs,)),
+            dma((pairs, tiles)),
+            dma((pairs, tiles)),
+            dma((pairs,)),
             dma((groups,)),
             dma((groups,)),
             dma((count,)),
             dma((count,)),
         ],
         compiler_params=pltpu.CompilerParams(
-            collective_id=0, has_side_effects=True, vmem_limit_bytes=48 * 1024 * 1024
+            collective_id=0, has_side_effects=True, vmem_limit_bytes=60 * 1024 * 1024
         ),
         cost_estimate=pl.CostEstimate(
             flops=2 * macs,
@@ -435,6 +547,7 @@
             transcendentals=0,
         ),
     )(factor, index, rhs_sep, rhs_local, diag_inv, codes, root_inv)
+    return local, sep.reshape(rhs_count, share)
 
 
 def fits(mesh, rhs_local, diag_inv, codes, root_inv):

time: 59.6 us -> 50.6 us (0.85)
  the two profiles are of different devices: /device:TPU:25 before, /device:TPU:0 now
where the time goes in v2:
time: 50.6 us; the launch traced here: 50.3 us
  Pallas kernels  42.6 us (84%)
  local copies, waits for them, and re-layouts  5.65 us (11%)
  between operations  1.29 us (3%)
  other arithmetic  0.77 us (2%)
    pallas_call x1, Pallas kernels, fused(): pl.pallas_call(functools.partial(kernel, groups, tiles), out_shape=(jax.S...  42.6 us
    unnamed x2, local copies, waits for them, and re-layouts  3.61 us

profile of v2, /device:TPU:0, one launch (start us, length us, event | category | flops | bytes accessed | tf_op | source)
XLA Modules:
  0.0 50.3 jit_solution(1755960570905559126)
XLA Ops:
  1.3 0.7 %fusion = f32[640]{0:T(1024)S(1)} fusion(f32[640]{0:T(1024)} %param.11, s32[]{:T(128)} %bitcast.4), kind=kLoop, calls=%fused_computation.1 | loop fusion | flops 1280 | bytes 5124 | tf_op jit(solution)/shard_map/mul | solution.py:489
  2.0 0.1 reshape.23
  2.1 0.6 %pad.8 = f32[8,128]{1,0:T(8,128)} pad(f32[8,80]{1,0:T(8,128)S(1)} %reshape.23, f32[]{:T(128)} %constant.2.clone.1), padding=0_0x0_48 | pad | bytes 6660 | tf_op jit(solution)/shard_map/jit(_pad)/pad | solution.py:490
  2.7 0.8 %reshape.25 = s32[8,80]{1,0:T(8,128)S(1)} reshape(s32[640]{0:T(1024)} %param.12) | data formatting | bytes 5120 | tf_op jit(solution)/shard_map/reshape | solution.py:493
  3.4 0.1 broadcast_subtract_fusion
  3.5 0.6 %pad.9 = s32[8,128]{1,0:T(8,128)} pad(s32[8,80]{1,0:T(8,128)S(1)} %broadcast_subtract_fusion, s32[]{:T(128)} %constant.7.clone.1), padding=0_0x0_48 | pad | bytes 6660 | tf_op jit(solution)/shard_map/jit(_pad)/pad | solution.py:492
  4.1 42.6 %shard_map.95 = (bf16[192,1536]{1,0:T(8,128)(2,1)}, f32[3,64,320]{2,1,0:T(8,128)}) custom-call(f32[1,1024]{1,0:T(1,128)} %bitcast.6, s32[8,1,128]{2,1,0:T(1,128)} %bitcast.7, bf16[192,320]{1,0:T(8,128)(2,1)} %rhs_sep_ref.1, bf16[192,1536]{1,0:T(8,128)(2,1)} %rhs_hbm.1, bf16[3,512,512]{2,1,0:T(8,128)(2,1)} %diag_hbm.1, bf16[640,1536]{1,0:T(8,128)(2,1)} %codes_hbm.1, ...), custom_call_target="tpu_custom_call" | custom-call | flops 1811939328 | bytes 6356992 | tf_op jit(solution)/shard_map/pallas_call | solution.py:499
  46.7 1.9 %copy.13 = bf16[192,1536]{1,0:T(8,128)(2,1)} copy(bf16[192,1536]{1,0:T(8,128)(2,1)} %get-tuple-element.8) | data formatting | bytes 1179648
  48.6 1.7 %copy.14 = f32[192,320]{1,0:T(8,128)} copy(f32[192,320]{1,0:T(8,128)} %bitcast.5) | data formatting | bytes 491520
  (1 shorter events, 0.0 us)

commit v3 on v2

--- a/solution.py
+++ b/solution.py
@@ -9,6 +9,7 @@
 
 LANES = 128
 ROWS = 16
+VMEM_BYTES = 54 * 1024 * 1024
 MESH = pl.DeviceIdType.MESH
 F32 = jnp.float32
 BF16 = jnp.bfloat16
@@ -55,15 +56,16 @@
 def kernel(
     groups,
     tiles,
-    factor_ref,
-    index_ref,
+    live_ref,
+    scales_ref,
+    places_ref,
     rhs_sep_ref,
     rhs_hbm,
     diag_hbm,
     codes_hbm,
     root_hbm,
-    out_ref,
-    sep_ref,
+    out_hbm,
+    sep_hbm,
     rhs,
     diag,
     codes,
@@ -81,6 +83,11 @@
     picked,
     pick_got,
     update,
+    factor_ref,
+    index_ref,
+    out_ref,
+    sep_ref,
+    store_sem,
     load_sem,
     code_sem,
     self_sem,
@@ -123,6 +130,10 @@
     def rows_of(group):
         return pl.ds(pl.multiple_of(group * ROWS, ROWS), ROWS)
 
+    def halves(b):
+        half = block_len // 2
+        return [(b * block_len + h * half, b * block_len + (h + 1) * half) for h in range(2)]
+
     def device(slot):
         return (lax.rem(slot, groups), slot // groups)
 
@@ -160,13 +171,28 @@
                 (LANES - per_share, codes.shape[1]), BF16
             )
 
+    all_rows = scales_ref.shape[0]
+    eight = (8, all_rows)
+    scales = jnp.broadcast_to(scales_ref[...][None, :], eight)
+    places = jnp.broadcast_to(places_ref[...][None, :], eight)
+    position = lax.broadcasted_iota(jnp.int32, eight, 1)
+    scales = jnp.where(position < live_ref[0], scales, 0.0)
+    filled = lane_index(8) < per_share
+    for j in range(tiles):
+        shift = (all_rows - j * per_share) % all_rows
+        turned = [pltpu.roll(x, shift, 1) if shift else x for x in (scales, places)]
+        factor_ref[:, j * LANES : (j + 1) * LANES] = jnp.where(filled, turned[0][:, :LANES], 0.0)[:1]
+        index_ref[j] = jnp.where(filled, turned[1][:, :LANES] - j * share, -1)[:1]
+
     loads[0].wait()
     for b in range(per_dev):
         loads[1 + b].wait()
-        cols = slice(b * block_len, (b + 1) * block_len)
-        forward[:, cols] = jnp.dot(
-            rhs[:, cols], diag[b], preferred_element_type=F32
-        ).astype(BF16)
+        for low, high in halves(b):
+            forward[:, low:high] = jnp.dot(
+                rhs[:, b * block_len : high],
+                diag[b, : high - b * block_len, low - b * block_len : high - b * block_len],
+                preferred_element_type=F32,
+            ).astype(BF16)
 
     pl.semaphore_wait(barrier, count - 1)
 
@@ -433,13 +459,6 @@
         return carry
 
     lax.fori_loop(0, pairs, gather_picks, 0)
-    for b in range(per_dev):
-        cols = slice(b * block_len, (b + 1) * block_len)
-        misfit = (forward[:, cols].astype(F32) - update[:, cols]).astype(BF16)
-        out_ref[:, cols] = lax.dot_general(
-            misfit, diag[b], NT, preferred_element_type=F32
-        ).astype(BF16)
-
     own_sep.wait()
 
     def sep_done(k, carry):
@@ -449,6 +468,24 @@
         return carry
 
     lax.fori_loop(1, groups, sep_done, 0)
+
+    stores = [pltpu.make_async_copy(sep_ref, sep_hbm, store_sem.at[per_dev])]
+    stores[0].start()
+    for b in range(per_dev):
+        cols = slice(b * block_len, (b + 1) * block_len)
+        misfit = (forward[:, cols].astype(F32) - update[:, cols]).astype(BF16)
+        for low, high in halves(b):
+            first = low - b * block_len
+            out_ref[:, low:high] = lax.dot_general(
+                misfit[:, first:],
+                diag[b, first : high - b * block_len, first:],
+                NT,
+                preferred_element_type=F32,
+            ).astype(BF16)
+        stores.append(
+            pltpu.make_async_copy(out_ref.at[:, cols], out_hbm.at[:, cols], store_sem.at[b])
+        )
+        stores[-1].start()
 
     def sent(k, carry):
         peer = lax.rem(mine + k, count)
@@ -471,6 +508,25 @@
                 return carry
 
             lax.fori_loop(1, 2 * pair + 2, fsep_sent, 0)
+
+    for store in stores:
+        store.wait()
+
+
+def hand_over(local_in, sep_in, local_out, sep_out, sems):
+    parts = sems.shape[0] // 2
+    copies = []
+    for source, dest in ((local_in, local_out), (sep_in, sep_out)):
+        rows = source.shape[0] // parts
+        for part in range(parts):
+            these = pl.ds(part * rows, rows)
+            copies.append(
+                pltpu.make_async_copy(source.at[these], dest.at[these], sems.at[len(copies)])
+            )
+    for copy in copies:
+        copy.start()
+    for copy in copies:
+        copy.wait()
 
 
 def fused(rhs_local, diag_inv, codes, row_scales, sep_index, live_rows, rhs_sep, root_inv):
@@ -484,15 +540,8 @@
     rpg = rhs_count // groups
     subs, pairs = rpg // ROWS, tiles // 2
     packed = pl.cdiv(subs * per_share, LANES) * LANES
-    pad = ((0, 0), (0, LANES - per_share))
-    positions = jnp.arange(coupled_rows, dtype=jnp.int32)
-    factor = row_scales * (positions < live_rows[0]).astype(F32)
-    factor = jnp.pad(factor.reshape(tiles, per_share), pad).reshape(1, tiles * LANES)
-    bases = (jnp.arange(tiles, dtype=jnp.int32) * share)[:, None]
-    index = jnp.pad(
-        sep_index.reshape(tiles, per_share) - bases, pad, constant_values=-1
-    ).reshape(tiles, 1, LANES)
     vmem = pl.BlockSpec(memory_space=pltpu.VMEM)
+    scalar = pl.BlockSpec(memory_space=pltpu.SMEM)
     anywhere = pl.BlockSpec(memory_space=pl.ANY)
     dma = pltpu.SemaphoreType.DMA
     macs = rhs_count * local_len * 2 * (block_len + tiles * LANES)
@@ -502,8 +551,8 @@
             jax.ShapeDtypeStruct((rhs_count, local_len), BF16),
             jax.ShapeDtypeStruct((subs, groups * ROWS, share), F32),
         ),
-        in_specs=[vmem, vmem, vmem, anywhere, anywhere, anywhere, anywhere],
-        out_specs=(vmem, vmem),
+        in_specs=[scalar, vmem, vmem, vmem, anywhere, anywhere, anywhere, anywhere],
+        out_specs=(anywhere, anywhere),
         scratch_shapes=[
             pltpu.VMEM((rhs_count, local_len), BF16),
             pltpu.VMEM(diag_inv.shape, BF16),
@@ -522,6 +571,11 @@
             pltpu.VMEM((count, ROWS, packed), BF16),
             pltpu.VMEM((tiles, groups * ROWS, packed), BF16),
             pltpu.VMEM((rhs_count, local_len), F32),
+            pltpu.VMEM((1, tiles * LANES), F32),
+            pltpu.VMEM((tiles, 1, LANES), jnp.int32),
+            pltpu.VMEM((rhs_count, local_len), BF16),
+            pltpu.VMEM((subs, groups * ROWS, share), F32),
+            dma((1 + per_dev,)),
             dma((2 + per_dev,)),
             dma((tiles,)),
             dma((4,)),
@@ -539,15 +593,35 @@
             dma((count,)),
         ],
         compiler_params=pltpu.CompilerParams(
-            collective_id=0, has_side_effects=True, vmem_limit_bytes=60 * 1024 * 1024
+            collective_id=0, has_side_effects=True, vmem_limit_bytes=VMEM_BYTES
         ),
         cost_estimate=pl.CostEstimate(
             flops=2 * macs,
             bytes_accessed=2 * (diag_inv.size + codes.size + root_inv.size + 2 * rhs_local.size),
             transcendentals=0,
         ),
-    )(factor, index, rhs_sep, rhs_local, diag_inv, codes, root_inv)
-    return local, sep.reshape(rhs_count, share)
+    )(
+        live_rows,
+        row_scales,
+        sep_index,
+        rhs_sep,
+        rhs_local,
+        diag_inv,
+        codes,
+        root_inv,
+    )
+    sep = sep.reshape(rhs_count, share)
+    return pl.pallas_call(
+        hand_over,
+        out_shape=(
+            jax.ShapeDtypeStruct(local.shape, BF16),
+            jax.ShapeDtypeStruct(sep.shape, F32),
+        ),
+        in_specs=[anywhere, anywhere],
+        out_specs=(anywhere, anywhere),
+        scratch_shapes=[dma((2 * subs,))],
+        compiler_params=pltpu.CompilerParams(vmem_limit_bytes=VMEM_BYTES),
+    )(local, sep)
 
 
 def fits(mesh, rhs_local, diag_inv, codes, root_inv):
@@ -561,7 +635,7 @@
         and per_share % ROWS == 0
         and per_share <= LANES
         and share % (LANES // 2) == 0
-        and diag_inv.shape[1] % LANES == 0
+        and diag_inv.shape[1] % (2 * LANES) == 0 and codes.shape[0] // (groups * tiles) % LANES == 0
     )
 
 def selector(offsets, share_len):

time: 50.6 us -> 71.3 us (1.41)
  Pallas kernels: 42.6 us -> 69.9 us
  local copies, waits for them, and re-layouts: 5.65 us -> 0 us
  other arithmetic: 0.77 us -> 0 us
    pallas_call x0 -> x1, Pallas kernels: none -> 28 us  [fused(): pl.pallas_call(hand_over, out_shape=(jax.ShapeDtypeStruct(local.shape, BF...]
    unnamed x2 -> x0, local copies, waits for them, and re-layouts: 3.61 us -> none
    pad x2 -> x0, local copies, waits for them, and re-layouts: 1.2 us -> none  [the longest x1 0.6 us: fused(): jnp.pad(factor.reshape(tiles, per_share), pad).reshape(1, tiles * LANES)]
    reshape x2 -> x0, local copies, waits for them, and re-layouts: 0.83 us -> none  [the longest x1 0.76 us: fused(): sep_index.reshape(tiles, per_share) - bases]
where the time goes in v3:
time: 71.3 us; the launch traced here: 71.2 us
  Pallas kernels  69.9 us (98%)
  between operations  1.29 us (2%)
    pallas_call x1, Pallas kernels, fused(): pl.pallas_call(functools.partial(kernel, groups, tiles), out_shape=(jax.S...  41.9 us
    pallas_call x1, Pallas kernels, fused(): pl.pallas_call(hand_over, out_shape=(jax.ShapeDtypeStruct(local.shape, BF...  28 us

profile of v3, /device:TPU:0, one launch (start us, length us, event | category | flops | bytes accessed | tf_op | source)
XLA Modules:
  0.0 71.2 jit_solution(9427930683970682629)
XLA Ops:
  1.3 41.9 %shard_map.95 = (bf16[192,1536]{1,0:T(8,128)(2,1)}, f32[3,64,320]{2,1,0:T(8,128)}) custom-call(s32[1]{0:T(128)S(6)} %copy.10.live_ref, f32[640]{0:T(1024)} %scales_ref.1, s32[640]{0:T(1024)} %places_ref.1, bf16[192,320]{1,0:T(8,128)(2,1)} %rhs_sep_ref.1, bf16[192,1536]{1,0:T(8,128)(2,1)} %rhs_hbm.1, bf16[3,512,512]{2,1,0:T(8,128)(2,1)} %diag_hbm.1, ...), custom_call_target="tpu_custom_call" | custom-call | flops 1811939328 | bytes 6356992 | tf_op jit(solution)/shard_map/pallas_call | solution.py:548
  43.2 28.0 %shard_map.96 = (bf16[192,1536]{1,0:T(8,128)(2,1)}, f32[192,320]{1,0:T(8,128)}) custom-call(bf16[192,1536]{1,0:T(8,128)(2,1)} %get-tuple-element.4.local_in, f32[192,320]{1,0:T(8,128)} %bitcast.1), custom_call_target="tpu_custom_call" | custom-call | tf_op jit(solution)/shard_map/pallas_call | solution.py:614

commit v4 on v3

--- a/solution.py
+++ b/solution.py
@@ -432,6 +432,27 @@
     own_sep = pltpu.make_async_copy(solved, sep_ref.at[:, rows_of(g)], self_sem.at[3])
     own_sep.start()
 
+    def early_sent(k, carry):
+        peer = lax.rem(mine + k, count)
+        index_copy(peer, mine).wait_send()
+        term_copy(peer, mine).wait_send()
+        return carry
+
+    lax.fori_loop(1, count, early_sent, 0)
+    for pair in range(pairs):
+
+        @pl.when(jnp.logical_and(t < 2 * pair + 2, t != owner_of(pair)))
+        def _():
+            part_copy(pair, t).wait_send()
+
+        @pl.when(t == owner_of(pair))
+        def _():
+            def fsep_sent(k, carry):
+                fsep_copy(pair, lax.rem(t + k, 2 * pair + 2)).wait_send()
+                return carry
+
+            lax.fori_loop(1, 2 * pair + 2, fsep_sent, 0)
+
     own_pick.wait()
     update[...] = jnp.zeros_like(update)
 
@@ -488,45 +509,35 @@
         stores[-1].start()
 
     def sent(k, carry):
-        peer = lax.rem(mine + k, count)
-        index_copy(peer, mine).wait_send()
-        term_copy(peer, mine).wait_send()
-        pick_copy(peer, mine).wait_send()
+        pick_copy(lax.rem(mine + k, count), mine).wait_send()
         return carry
 
     lax.fori_loop(1, count, sent, 0)
-    for pair in range(pairs):
-
-        @pl.when(jnp.logical_and(t < 2 * pair + 2, t != owner_of(pair)))
-        def _():
-            part_copy(pair, t).wait_send()
-
-        @pl.when(t == owner_of(pair))
-        def _():
-            def fsep_sent(k, carry):
-                fsep_copy(pair, lax.rem(t + k, 2 * pair + 2)).wait_send()
-                return carry
-
-            lax.fori_loop(1, 2 * pair + 2, fsep_sent, 0)
-
     for store in stores:
         store.wait()
 
 
-def hand_over(local_in, sep_in, local_out, sep_out, sems):
-    parts = sems.shape[0] // 2
-    copies = []
-    for source, dest in ((local_in, local_out), (sep_in, sep_out)):
+def hand_over(local_in, sep_in, local_out, sep_out, local_held, sep_held, in_sems, out_sems):
+    parts = in_sems.shape[0] // 2
+    takes, gives = [], []
+    for source, held, dest in (
+        (local_in, local_held, local_out),
+        (sep_in, sep_held, sep_out),
+    ):
         rows = source.shape[0] // parts
         for part in range(parts):
-            these = pl.ds(part * rows, rows)
-            copies.append(
-                pltpu.make_async_copy(source.at[these], dest.at[these], sems.at[len(copies)])
+            these, pos = pl.ds(part * rows, rows), len(takes)
+            takes.append(
+                pltpu.make_async_copy(source.at[these], held.at[these], in_sems.at[pos])
             )
-    for copy in copies:
-        copy.start()
-    for copy in copies:
-        copy.wait()
+            gives.append(pltpu.make_async_copy(held.at[these], dest.at[these], out_sems.at[pos]))
+    for take in takes:
+        take.start()
+    for take, give in zip(takes, gives):
+        take.wait()
+        give.start()
+    for give in gives:
+        give.wait()
 
 
 def fused(rhs_local, diag_inv, codes, row_scales, sep_index, live_rows, rhs_sep, root_inv):
@@ -619,7 +630,12 @@
         ),
         in_specs=[anywhere, anywhere],
         out_specs=(anywhere, anywhere),
-        scratch_shapes=[dma((2 * subs,))],
+        scratch_shapes=[
+            pltpu.VMEM(local.shape, BF16),
+            pltpu.VMEM(sep.shape, F32),
+            dma((2 * subs,)),
+            dma((2 * subs,)),
+        ],
         compiler_params=pltpu.CompilerParams(vmem_limit_bytes=VMEM_BYTES),
     )(local, sep)
 

time: 71.3 us -> 45.4 us (0.64)
  Pallas kernels: 69.9 us -> 43.9 us
    pallas_call x1, Pallas kernels: 28 us -> 1.99 us  [fused(): pl.pallas_call(hand_over, out_shape=(jax.ShapeDtypeStruct(local.shape, BF...]
where the time goes in v4:
time: 45.4 us; the launch traced here: 45.2 us
  Pallas kernels  43.9 us (97%)
  between operations  1.29 us (3%)
    pallas_call x1, Pallas kernels, fused(): pl.pallas_call(functools.partial(kernel, groups, tiles), out_shape=(jax.S...  41.9 us
    pallas_call x1, Pallas kernels, fused(): pl.pallas_call(hand_over, out_shape=(jax.ShapeDtypeStruct(local.shape, BF...  1.99 us

profile of v4, /device:TPU:0, one launch (start us, length us, event | category | flops | bytes accessed | tf_op | source)
XLA Modules:
  0.0 45.2 jit_solution(3884353203568920373)
XLA Ops:
  1.3 41.9 %shard_map.95 = (bf16[192,1536]{1,0:T(8,128)(2,1)}, f32[3,64,320]{2,1,0:T(8,128)}) custom-call(s32[1]{0:T(128)S(6)} %copy.10.live_ref, f32[640]{0:T(1024)} %scales_ref.1, s32[640]{0:T(1024)} %places_ref.1, bf16[192,320]{1,0:T(8,128)(2,1)} %rhs_sep_ref.1, bf16[192,1536]{1,0:T(8,128)(2,1)} %rhs_hbm.1, bf16[3,512,512]{2,1,0:T(8,128)(2,1)} %diag_hbm.1, ...), custom_call_target="tpu_custom_call" | custom-call | flops 1811939328 | bytes 6356992 | tf_op jit(solution)/shard_map/pallas_call | solution.py:559
  43.2 2.0 %shard_map.96 = (bf16[192,1536]{1,0:T(8,128)(2,1)}, f32[192,320]{1,0:T(8,128)}) custom-call(bf16[192,1536]{1,0:T(8,128)(2,1)} %get-tuple-element.4.local_in, f32[192,320]{1,0:T(8,128)} %bitcast.1), custom_call_target="tpu_custom_call" | custom-call | tf_op jit(solution)/shard_map/pallas_call | solution.py:625
